TPU v7x, 128 devices: a whole 4x4x4 slice. The times are simulated.
128 devices in a mesh: seq: 128 (over y, x, z, core).
Axes of the slice: x: 4, y: 4, z: 4, core: 2. Of those that a mesh axis runs over, the one named last changes fastest.
Arguments:
- queries: bfloat16 [131072, 1024], P('seq'), may hold values from -8 to 8, as said below
- keys: bfloat16 [131072, 1024], P('seq'), may hold values from -8 to 8
- values: bfloat16 [131072, 1024], P('seq'), may hold values from -6 to 6
- w_out: bfloat16 [1024, 2048], replicated, may hold values from -0.1875 to 0.1875
Outputs:
- output: bfloat16 [131072, 2048], P('seq')
Inputs may be any that keep to these rules, and one draw needn't show every extreme that they name: `queries`: query entries lie in the range.
All inputs are finite; a program needn't handle non-finite values.
Results may differ from a plain program's by a relative error of at most 0.0023.
The roundings to bfloat16 on the way count: a program that leaves them out, or rounds other values in their place, can miss the bound.
Values may be sent and summed in bfloat16 or wider, within the bound.
A program may use at most 128 MiB of HBM per device.

v0:
```python
import functools
import math

import jax
import jax.numpy as jnp
from jax import lax
from jax.experimental import pallas as pl
from jax.experimental.pallas import tpu as pltpu
from jax.sharding import PartitionSpec as P

MESH = pl.DeviceIdType.MESH
HEAD = 128
PAIRS = 4
WIDE = 256
NEG = -1e30
C2 = HEAD ** -0.5 * math.log2(math.e)
BF = jnp.bfloat16
F32 = jnp.float32


def nt_dot(a, b):
    return lax.dot_general(a, b, (((1,), (1,)), ((), ())), preferred_element_type=F32)


def dot(a, b):
    return lax.dot_general(a, b, (((1,), (0,)), ((), ())), preferred_element_type=F32)


def coarse_term(q, k, v, level, flag):
    unit = 4.0 ** -level
    s = nt_dot(q, k)
    m = jnp.max(s, axis=1, keepdims=True)
    p = jnp.exp2((s - m) * (C2 * unit))
    num = dot(p.astype(BF), v)
    total = jnp.broadcast_to(jnp.sum(p, axis=1, keepdims=True) * 2.0 ** level, num.shape)
    peak = jnp.broadcast_to(m * unit, num.shape)
    if flag is None:
        return num, peak, total
    return jnp.where(flag, num, 0.0), jnp.where(flag, peak, NEG), jnp.where(flag, total, 0.0)


def merge(a, b):
    top = jnp.maximum(a[1], b[1])
    fa = jnp.exp2((a[1] - top) * C2)
    fb = jnp.exp2((b[1] - top) * C2)
    return fa * a[0] + fb * b[0], top, fa * a[2] + fb * b[2]


def widen(state, ref, times, start=0):
    rows = state[0].shape[0]
    for plane, value in enumerate(state):
        for r in range(times):
            ref[plane, pl.ds(start + r, rows, stride=times), :] = value
    return tuple(ref[i, pl.ds(start, rows * times), :] for i in range(3))


def local_block(q, k, v, init, bias, half):
    s = [nt_dot(q, k[i * 256:(i + 1) * 256]) for i in range(half + 1)]
    s[half] = s[half] + bias
    m = init[1]
    for item in s:
        m = jnp.maximum(m, jnp.max(item, axis=1, keepdims=True))
    m2 = jnp.concatenate([m, m], axis=1)
    f = jnp.exp2((init[1] - m) * C2)
    num, total = f * init[0], f * init[2]
    sums = None
    for i, item in enumerate(s):
        p = jnp.exp2((item - m2) * C2)
        num = num + dot(p.astype(BF), v[i * 256:(i + 1) * 256])
        sums = p if sums is None else sums + p
    return num, m, total + jnp.sum(sums, axis=1, keepdims=True)


def kernel(q_hbm, k_hbm, v_hbm, att_hbm, qb, kb, vb, pool, bias,
           kv1, q1, kv2, q2, r2, kv3, q3, r3, kv4, q4, r4,
           ts, rt, xs, r5, r6, r7, r8, cs, cr, wide, base, outb,
           load_sem, out_sem, s2, g2, s3, g3, y3, z3, s4, g4, y4, z4,
           sa, ga, sb, gb, sc, gc):
    me = lax.axis_index("seq")
    core = me & 1
    own = me & 7
    octet = me - own

    def bit(i):
        return (me >> i) & 1

    def load(hp, t):
        src = (k_hbm, v_hbm, q_hbm)[t]
        dst = (kb, vb, qb)[t]
        cols = pl.ds(pl.multiple_of(hp * WIDE, WIDE), WIDE)
        return pltpu.make_async_copy(src.at[:, cols], dst.at[hp], load_sem.at[hp, t])

    for hp in range(PAIRS):
        for t in range(3):
            load(hp, t).start()

    barrier = pltpu.get_barrier_semaphore()
    masks = list(range(1, 8)) + [8 * o for o in range(1, 16)]

    def greet(i, _):
        mask = jnp.where(i < 8, i, (i - 7) * 8)
        pl.semaphore_signal(barrier, inc=1, device_id=(me ^ mask,), device_id_type=MESH)
        return 0

    lax.fori_loop(1, 23, greet, 0)

    row = lax.broadcasted_iota(jnp.int32, (304, WIDE), 0)
    col = lax.broadcasted_iota(jnp.int32, (304, WIDE), 1)
    tail = row >= 240
    shift = jnp.where(row < 128, 1, jnp.where(row < 192, 2, jnp.where(row < 224, 3, 4)))
    off = jnp.where(row < 128, row, jnp.where(row < 192, row - 128, jnp.where(row < 224, row - 192, row - 224)))
    t = row - 240
    shift_t = jnp.where(t < 32, 5, jnp.where(t < 48, 6, jnp.where(t < 56, 7, 8)))
    off_t = jnp.where(t < 32, t, jnp.where(t < 48, t - 32, jnp.where(t < 56, t - 48, t - 56)))
    shift = jnp.where(tail, shift_t, shift)
    off = jnp.where(tail, off_t, off)
    for i in range(4):
        at = jnp.where(tail, col + 256 * i, col)
        pool[i] = jnp.where((at >> shift) == off, 1.0, 0.0).astype(BF)
    r_i = lax.broadcasted_iota(jnp.int32, (256, 256), 0)
    c_i = lax.broadcasted_iota(jnp.int32, (256, 256), 1)
    bias[...] = jnp.where(c_i <= r_i, 0.0, NEG)

    tr = lax.broadcasted_iota(jnp.int32, (64, WIDE), 0)
    side = jnp.where(tr < 32, bit(3), jnp.where(tr < 48, bit(4), jnp.where(tr < 56, bit(5), bit(6))))

    pl.semaphore_wait(barrier, len(masks))

    def copy_to(src, dst, send, recv, device):
        return pltpu.make_async_remote_copy(src_ref=src, dst_ref=dst, send_sem=send, recv_sem=recv,
                                            device_id=(device,), device_id_type=MESH)

    def send2(hp):
        return copy_to(kv2.at[hp], r2.at[hp], s2.at[hp], g2.at[hp], me ^ 1)

    def send3(hp):
        return copy_to(kv3.at[hp], r3.at[hp, core], s3.at[hp], g3.at[hp], me ^ 2)

    def relay3(hp):
        return copy_to(r3.at[hp, core], r3.at[hp, core], y3.at[hp], z3.at[hp], me ^ 1)

    def send4(hp, j):
        mask = 4 + 2 * j
        return copy_to(kv4.at[hp], r4.at[hp, core, bit(1)], s4.at[hp, j], g4.at[hp, j], me ^ mask)

    def recv4(hp, j):
        slot = bit(1) ^ j
        mask = 4 + 2 * j
        return copy_to(kv4.at[hp], r4.at[hp, core, slot], s4.at[hp, j], g4.at[hp, j], me ^ mask)

    def relay4(hp):
        return copy_to(r4.at[hp, core], r4.at[hp, core], y4.at[hp], z4.at[hp], me ^ 1)

    def send_a(h):
        return copy_to(ts.at[h], rt.at[own], sa.at[h], ga.at[own], octet + h)

    def recv_a(h):
        return copy_to(ts.at[h], rt.at[h], sa.at[h], ga.at[h], octet + h)

    def send_c(h):
        return copy_to(cs.at[h], cr.at[own], sc.at[h], gc.at[own], octet + h)

    def recv_c(h):
        return copy_to(cs.at[h], cr.at[h], sc.at[h], gc.at[h], octet + h)

    def copy_b(level, i):
        count = 256 >> (level - 5)
        start = (0, 256, 384, 448)[level - 5]
        n = 1 << (level - 5)
        dst = (r5, r6, r7, r8)[level - 5]
        slot = n - 1 + i
        mask = 8 * (n + i)
        return copy_to(xs.at[:, pl.ds(start, count)], dst.at[i], sb.at[slot], gb.at[slot], me ^ mask)

    def pool_pair(hp, _):
        tails = []
        for t in range(3):
            load(hp, t).wait()
            src = (kb, vb, qb)[t]
            acc = None
            for i in range(4):
                y = dot(pool[i], src[hp, i * 256:(i + 1) * 256, :])
                yb = y[:240].astype(BF)
                if t < 2:
                    if i < 2:
                        kv1[hp, t, i * 128:(i + 1) * 128, :] = yb[:128]
                    kv2[hp, t, i * 64:(i + 1) * 64, :] = yb[128:192]
                    kv3[hp, t, i * 32:(i + 1) * 32, :] = yb[192:224]
                    kv4[hp, t, i * 16:(i + 1) * 16, :] = yb[224:240]
                else:
                    if i >= 2:
                        q1[hp, (i - 2) * 128:(i - 1) * 128, :] = yb[:128]
                    q2[hp, i * 64:(i + 1) * 64, :] = yb[128:192]
                    q3[hp, i * 32:(i + 1) * 32, :] = yb[192:224]
                    q4[hp, i * 16:(i + 1) * 16, :] = yb[224:240]
                acc = y[240:] if acc is None else acc + y[240:]
            tails.append(acc)
        first = jnp.where(side == 0, tails[0], tails[2]).astype(BF)
        second = tails[1].astype(BF)
        for e in range(2):
            h = 2 * hp + e
            ts[h, 0] = first[:, e * HEAD:(e + 1) * HEAD]
            ts[h, 1] = second[:, e * HEAD:(e + 1) * HEAD]

            @pl.when(h != own)
            def _():
                send_a(h).start()

        @pl.when(bit(2) == 0)
        def _():
            send4(hp, 0).start()
            send4(hp, 1).start()

        @pl.when(bit(1) == 0)
        def _():
            send3(hp).start()

        @pl.when(core == 0)
        def _():
            send2(hp).start()

        return 0

    lax.fori_loop(0, PAIRS, pool_pair, 0)
    rt[own] = ts[own]

    def wait_a():
        def one(h, _):
            @pl.when(h != own)
            def _():
                recv_a(h).wait_recv()
            return 0
        lax.fori_loop(0, 8, one, 0)
        i = lax.broadcasted_iota(jnp.int32, (512, 512), 0)
        j = lax.broadcasted_iota(jnp.int32, (512, 512), 1)
        i6, i7, i8 = i - 256, i - 384, i - 448
        at = jnp.where(i < 256, (i >> 5) * 64 + (i & 31),
             jnp.where(i < 384, (i6 >> 4) * 64 + 32 + (i6 & 15),
             jnp.where(i < 448, (i7 >> 3) * 64 + 48 + (i7 & 7),
             jnp.where(i < 480, (i8 >> 2) * 64 + 56 + (i8 & 3), -1))))
        move = jnp.where(at == j, 1.0, 0.0).astype(BF)
        both = jnp.concatenate([rt[:, 0].reshape(512, HEAD), rt[:, 1].reshape(512, HEAD)], axis=1)
        x = dot(move, both).astype(BF)
        xs[0] = x[:, :HEAD]
        xs[1] = x[:, HEAD:]
        for level in range(8, 4, -1):
            n = 1 << (level - 5)

            @pl.when(bit(level - 2) == 0)
            def _():
                for i in range(n):
                    copy_b(level, i).start()

    def wait_b():
        for level in range(8, 4, -1):
            n = 1 << (level - 5)

            @pl.when(bit(level - 2) == 1)
            def _():
                for i in range(n):
                    copy_b(level, i).wait_recv()
        terms = []
        for level, ref in ((8, r8), (7, r7), (6, r6), (5, r5)):
            start = (0, 256, 384, 448)[level - 5]
            rows = 256 >> (level - 5)
            terms.append(coarse_term(xs[0, start:start + rows, :], ref[:, 0].reshape(256, HEAD),
                                     ref[:, 1].reshape(256, HEAD), level, bit(level - 2) == 1))
        state = terms[0]
        for term in terms[1:]:
            state = merge(widen(state, wide.at[0], 2), term)
        lane = lax.broadcasted_iota(jnp.int32, (256, HEAD), 1)
        cs[:, 0] = state[0].reshape(8, 32, HEAD)
        cs[:, 1] = jnp.where(lane < 64, state[1], state[2]).reshape(8, 32, HEAD)
        cr[own] = cs[own]

        def one(h, _):
            @pl.when(h != own)
            def _():
                send_c(h).start()
            return 0
        lax.fori_loop(0, 8, one, 0)

    def local_pair(hp, _):
        @pl.when(core == 1)
        def _():
            send2(hp).wait_recv()
        for e in range(2):
            cols = slice(e * HEAD, (e + 1) * HEAD)
            two = coarse_term(q2[hp, :, cols], r2[hp, 0, :, cols], r2[hp, 1, :, cols], 2, core == 1)
            one = coarse_term(q1[hp, :, cols], kv1[hp, 0, :, cols], kv1[hp, 1, :, cols], 1, None)
            w = wide.at[e]
            low = tuple(x[:128] for x in two)
            high = tuple(x[128:] for x in two)
            init0 = widen(low, w, 4)
            init1 = widen(merge(widen(high, w, 2, 512), one), w, 2, 512)
            for seg, init in ((0, init0), (1, init1)):
                k = kb[hp, seg * 512:(seg + 1) * 512, cols]
                v = vb[hp, seg * 512:(seg + 1) * 512, cols]
                for half in range(2):
                    at = seg * 512 + half * 256
                    q = qb[hp, at:at + 256, cols]
                    part = tuple(x[half * 256:(half + 1) * 256] for x in init)
                    res = local_block(q, k, v, part, bias[...], half)
                    for i in range(3):
                        base[2 * hp + e, i, at:at + 256, :] = res[i]

        @pl.when(hp == 0)
        def _():
            wait_a()

        @pl.when(hp == 2)
        def _():
            wait_b()
        return 0

    lax.fori_loop(0, PAIRS, local_pair, 0)

    def recv_c_all(h, _):
        @pl.when(h != own)
        def _():
            recv_c(h).wait_recv()
        return 0

    lax.fori_loop(0, 8, recv_c_all, 0)

    def out_copy(hp):
        cols = pl.ds(pl.multiple_of(hp * WIDE, WIDE), WIDE)
        return pltpu.make_async_copy(outb.at[hp], att_hbm.at[:, cols], out_sem.at[hp])

    def final_pair(step, _):
        @pl.when(step < PAIRS)
        def _():
            @pl.when(bit(2) == 1)
            def _():
                recv4(step, 0).wait_recv()
                recv4(step, 1).wait_recv()
                relay4(step).start()

            @pl.when(bit(1) == 1)
            def _():
                send3(step).wait_recv()
                relay3(step).start()

        @pl.when(step > 0)
        def _():
            hp = step - 1

            @pl.when(bit(2) == 1)
            def _():
                copy_to(r4.at[hp, 1 - core], r4.at[hp, 1 - core], y4.at[hp], z4.at[hp], me ^ 1).wait_recv()

            @pl.when(bit(1) == 1)
            def _():
                copy_to(r3.at[hp, 1 - core], r3.at[hp, 1 - core], y3.at[hp], z3.at[hp], me ^ 1).wait_recv()

            for e in range(2):
                cols = slice(e * HEAD, (e + 1) * HEAD)
                h = 2 * hp + e
                w = wide.at[e]
                three = coarse_term(q3[hp, :, cols], r3[hp, :, 0, :, cols].reshape(256, HEAD),
                                    r3[hp, :, 1, :, cols].reshape(256, HEAD), 3, bit(1) == 1)
                four = coarse_term(q4[hp, :, cols], r4[hp, :, :, 0, :, cols].reshape(256, HEAD),
                                   r4[hp, :, :, 1, :, cols].reshape(256, HEAD), 4, bit(2) == 1)
                stats = cr[h, 1]
                five = (cr[h, 0], jnp.broadcast_to(stats[:, :1], (32, HEAD)),
                        jnp.broadcast_to(stats[:, 64:65], (32, HEAD)))
                state = merge(widen(five, w, 2), four)
                state = merge(widen(state, w, 2), three)
                state = widen(state, w, 8)
                num, _, total = merge(tuple(base[h, i] for i in range(3)), state)
                outb[hp, :, cols] = (num / total).astype(BF)
            out_copy(hp).start()
        return 0

    lax.fori_loop(0, PAIRS + 1, final_pair, 0)

    def drain(hp, _):
        out_copy(hp).wait()

        @pl.when(core == 0)
        def _():
            send2(hp).wait_send()

        @pl.when(bit(1) == 0)
        def _():
            send3(hp).wait_send()

        @pl.when(bit(1) == 1)
        def _():
            relay3(hp).wait_send()

        @pl.when(bit(2) == 0)
        def _():
            send4(hp, 0).wait_send()
            send4(hp, 1).wait_send()

        @pl.when(bit(2) == 1)
        def _():
            relay4(hp).wait_send()
        return 0

    lax.fori_loop(0, PAIRS, drain, 0)

    def drain_octet(h, _):
        @pl.when(h != own)
        def _():
            send_a(h).wait_send()
            send_c(h).wait_send()
        return 0

    lax.fori_loop(0, 8, drain_octet, 0)
    for level in range(8, 4, -1):
        n = 1 << (level - 5)

        @pl.when(bit(level - 2) == 0)
        def _():
            for i in range(n):
                copy_b(level, i).wait_send()


def attend(queries, keys, values):
    count, width = queries.shape
    vm = lambda *shape: pltpu.VMEM(shape, BF)
    vf = lambda *shape: pltpu.VMEM(shape, F32)
    dma = lambda *shape: pltpu.SemaphoreType.DMA(shape)
    scratch = [
        vm(4, 1024, 256), vm(4, 1024, 256), vm(4, 1024, 256),
        vm(4, 304, 256), vf(256, 256),
        vm(4, 2, 256, 256), vm(4, 256, 256),
        vm(4, 2, 256, 256), vm(4, 256, 256), vm(4, 2, 256, 256),
        vm(4, 2, 128, 256), vm(4, 128, 256), vm(4, 2, 2, 128, 256),
        vm(4, 2, 64, 256), vm(4, 64, 256), vm(4, 2, 2, 2, 64, 256),
        vm(8, 2, 64, 128), vm(8, 2, 64, 128), vm(2, 512, 128),
        vm(1, 2, 256, 128), vm(2, 2, 128, 128), vm(4, 2, 64, 128), vm(8, 2, 32, 128),
        vf(8, 2, 32, 128), vf(8, 2, 32, 128),
        vf(2, 3, 1024, 128), vf(8, 3, 1024, 128), vm(4, 1024, 256),
        dma(4, 3), dma(4),
        dma(4), dma(4),
        dma(4), dma(4), dma(4), dma(4),
        dma(4, 2), dma(4, 2), dma(4), dma(4),
        dma(8), dma(8), dma(15), dma(15), dma(8), dma(8),
    ]
    return pl.pallas_call(
        kernel,
        out_shape=jax.ShapeDtypeStruct((count, width), BF),
        in_specs=[pl.BlockSpec(memory_space=pl.ANY)] * 3,
        out_specs=pl.BlockSpec(memory_space=pl.ANY),
        scratch_shapes=scratch,
        compiler_params=pltpu.CompilerParams(
            collective_id=0, has_side_effects=True, vmem_limit_bytes=56 * 1024 * 1024
        ),
        name="hierarchical_attention",
    )(queries, keys, values)


def on_device(queries, keys, values, w_out):
    attended = attend(queries, keys, values)
    return jnp.dot(attended, w_out, preferred_element_type=F32).astype(BF)


def solution(mesh):
    return jax.shard_map(
        on_device,
        mesh=mesh,
        in_specs=(P("seq", None), P("seq", None), P("seq", None), P()),
        out_specs=P("seq", None),
        check_vma=False,
    )
```

profile of v0, /device:TPU:3, one launch (start us, length us, event | category | flops | bytes accessed | tf_op | source)
XLA Modules:
  0.0 54.9 jit_solution(9880063932717382410)
XLA Ops:
  0.0 0.0 copy-start
  0.0 47.3 %hierarchical_attention.1 = bf16[1024,1024]{1,0:T(8,128)(2,1)} custom-call(bf16[1024,1024]{1,0:T(8,128)(2,1)} %q_hbm.1, bf16[1024,1024]{1,0:T(8,128)(2,1)} %k_hbm.1, bf16[1024,1024]{1,0:T(8,128)(2,1)} %v_hbm.1), custom_call_target="tpu_custom_call" | custom-call | tf_op jit(solution)/shard_map/hierarchical_attention/pallas_call | solution.py:443
  47.3 0.0 copy-done
  47.3 7.6 %convolution_convert_fusion = bf16[1024,2048]{1,0:T(8,128)(2,1)} fusion(bf16[1024,1024]{1,0:T(8,128)(2,1)} %hierarchical_attention.1, bf16[1024,2048]{1,0:T(8,128)(2,1)S(1)} %copy-done), kind=kOutput, calls=%fused_computation | convolution fusion | flops 4297064448 | bytes 10485760 | tf_op jit(solution)/shard_map/dot_general | solution.py:458
Async XLA Ops:
  0.0 47.3 %copy-start = (bf16[1024,2048]{1,0:T(8,128)(2,1)S(1)}, bf16[1024,2048]{1,0:T(8,128)(2,1)}, u32[]{:S(2)}) copy-start(bf16[1024,2048]{1,0:T(8,128)(2,1)} %param.7) | copy-start | bytes 12582916
where the time goes:
time: 55.1 us; the launch traced here: 54.9 us
  Pallas kernels  47.3 us (86%)
  matrix products  7.61 us (14%)
    pallas_call x1, Pallas kernels, attend(): pl.pallas_call(kernel, out_shape=jax.ShapeDtypeStruct((count, width), BF)...  47.3 us
    dot_general x1, matrix products, on_device(): return jnp.dot(attended, w_out, preferred_element_type=F32).astype(BF)  7.61 us

commit v1 on v0

--- a/solution.py
+++ b/solution.py
@@ -26,17 +26,66 @@
     return lax.dot_general(a, b, (((1,), (0,)), ((), ())), preferred_element_type=F32)
 
 
-def coarse_term(q, k, v, level, flag):
-    unit = 4.0 ** -level
-    s = nt_dot(q, k)
-    m = jnp.max(s, axis=1, keepdims=True)
-    p = jnp.exp2((s - m) * (C2 * unit))
-    num = dot(p.astype(BF), v)
-    total = jnp.broadcast_to(jnp.sum(p, axis=1, keepdims=True) * 2.0 ** level, num.shape)
-    peak = jnp.broadcast_to(m * unit, num.shape)
-    if flag is None:
-        return num, peak, total
-    return jnp.where(flag, num, 0.0), jnp.where(flag, peak, NEG), jnp.where(flag, total, 0.0)
+def tile_scores(tile):
+    q, keys = tile["q"](), tile["k"]()
+    scores = [nt_dot(q, k) for k in keys]
+    if tile["bias"] is not None:
+        scores[-1] = scores[-1] + tile["bias"][...]
+    return scores
+
+
+def tile_probs(tile, scores):
+    scale = C2 * 4.0 ** -tile["level"]
+    peak = None
+    for s in scores:
+        top = jnp.max(s, axis=1, keepdims=True)
+        peak = top if peak is None else jnp.maximum(peak, top)
+    probs, total = [], None
+    for s in scores:
+        p = jnp.exp2((s - peak) * scale)
+        row = jnp.sum(p, axis=1, keepdims=True)
+        total = row if total is None else total + row
+        probs.append(p.astype(BF))
+    return probs, peak, total
+
+
+def tile_out(tile, probs, peak, total):
+    num = None
+    for p, v in zip(probs, tile["v"]()):
+        part = dot(p, v)
+        num = part if num is None else num + part
+    tile["sink"](num, peak, total)
+
+
+def run_tiles(tiles):
+    scores, probs = {}, {}
+    count = len(tiles)
+    for i in range(count + 2):
+        if i < count:
+            scores[i] = tile_scores(tiles[i])
+        if 1 <= i <= count:
+            probs[i - 1] = tile_probs(tiles[i - 1], scores.pop(i - 1))
+        if i >= 2:
+            tile_out(tiles[i - 2], *probs.pop(i - 2))
+
+
+def coarse_tile(level, q, k, v, flag, sink):
+    def done(num, peak, total):
+        peak = jnp.broadcast_to(peak * 4.0 ** -level, num.shape)
+        total = jnp.broadcast_to(total * 2.0 ** level, num.shape)
+        if flag is not None:
+            num = jnp.where(flag, num, 0.0)
+            peak = jnp.where(flag, peak, NEG)
+            total = jnp.where(flag, total, 0.0)
+        sink(num, peak, total)
+    return {"q": q, "k": lambda: [k()], "v": lambda: [v()], "bias": None, "level": level, "sink": done}
+
+
+def store(ref, *index):
+    def sink(*planes):
+        for i, plane in enumerate(planes):
+            ref[(*index, i)] = plane
+    return sink
 
 
 def merge(a, b):
@@ -51,30 +100,13 @@
     for plane, value in enumerate(state):
         for r in range(times):
             ref[plane, pl.ds(start + r, rows, stride=times), :] = value
-    return tuple(ref[i, pl.ds(start, rows * times), :] for i in range(3))
-
-
-def local_block(q, k, v, init, bias, half):
-    s = [nt_dot(q, k[i * 256:(i + 1) * 256]) for i in range(half + 1)]
-    s[half] = s[half] + bias
-    m = init[1]
-    for item in s:
-        m = jnp.maximum(m, jnp.max(item, axis=1, keepdims=True))
-    m2 = jnp.concatenate([m, m], axis=1)
-    f = jnp.exp2((init[1] - m) * C2)
-    num, total = f * init[0], f * init[2]
-    sums = None
-    for i, item in enumerate(s):
-        p = jnp.exp2((item - m2) * C2)
-        num = num + dot(p.astype(BF), v[i * 256:(i + 1) * 256])
-        sums = p if sums is None else sums + p
-    return num, m, total + jnp.sum(sums, axis=1, keepdims=True)
+    return tuple(ref[i, pl.ds(start, rows * times), :] for i in range(len(state)))
 
 
 def kernel(q_hbm, k_hbm, v_hbm, att_hbm, qb, kb, vb, pool, bias,
-           kv1, q1, kv2, q2, r2, kv3, q3, r3, kv4, q4, r4,
-           ts, rt, xs, r5, r6, r7, r8, cs, cr, wide, base, outb,
-           load_sem, out_sem, s2, g2, s3, g3, y3, z3, s4, g4, y4, z4,
+           kv1, q1, kv2, q2, r2, kv3, q3, r3, kv4, q4, r4, f4,
+           ts, rt, xs, r5, r6, r7, r8, cs, cr, wide, base, near, far, deep, outb,
+           load_sem, out_sem, s2, g2, s3, g3, y3, z3, s4, g4, h4, y4, z4,
            sa, ga, sb, gb, sc, gc):
     me = lax.axis_index("seq")
     core = me & 1
@@ -124,8 +156,6 @@
     tr = lax.broadcasted_iota(jnp.int32, (64, WIDE), 0)
     side = jnp.where(tr < 32, bit(3), jnp.where(tr < 48, bit(4), jnp.where(tr < 56, bit(5), bit(6))))
 
-    pl.semaphore_wait(barrier, len(masks))
-
     def copy_to(src, dst, send, recv, device):
         return pltpu.make_async_remote_copy(src_ref=src, dst_ref=dst, send_sem=send, recv_sem=recv,
                                             device_id=(device,), device_id_type=MESH)
@@ -139,14 +169,31 @@
     def relay3(hp):
         return copy_to(r3.at[hp, core], r3.at[hp, core], y3.at[hp], z3.at[hp], me ^ 1)
 
-    def send4(hp, j):
-        mask = 4 + 2 * j
-        return copy_to(kv4.at[hp], r4.at[hp, core, bit(1)], s4.at[hp, j], g4.at[hp, j], me ^ mask)
+    def send4(hp):
+        return copy_to(kv4.at[hp], r4.at[hp, core, bit(1)], s4.at[hp, 0], g4.at[hp, 0], me ^ 6)
 
     def recv4(hp, j):
-        slot = bit(1) ^ j
-        mask = 4 + 2 * j
-        return copy_to(kv4.at[hp], r4.at[hp, core, slot], s4.at[hp, j], g4.at[hp, j], me ^ mask)
+        return copy_to(kv4.at[hp], r4.at[hp, core, bit(1) ^ 1 ^ j], s4.at[hp, j], g4.at[hp, j], me ^ 6)
+
+    def lend4(hp):
+        return copy_to(kv4.at[hp], f4.at[hp], s4.at[hp, 1], h4.at[hp], me ^ 2)
+
+    def pass4(hp):
+        return copy_to(f4.at[hp], r4.at[hp, core, 1], s4.at[hp, 1], g4.at[hp, 1], me ^ 6)
+
+    def hand4(hp):
+        return copy_to(r4.at[hp, core, 0], r4.at[hp, core, 0], s4.at[hp, 0], g4.at[hp, 1], me ^ 2)
+
+    def forward4(hp):
+        @pl.when(own < 2)
+        def _():
+            lend4(hp).wait_recv()
+            pass4(hp).start()
+
+        @pl.when(own >= 6)
+        def _():
+            recv4(hp, 0).wait_recv()
+            hand4(hp).start()
 
     def relay4(hp):
         return copy_to(r4.at[hp, core], r4.at[hp, core], y4.at[hp], z4.at[hp], me ^ 1)
@@ -178,23 +225,37 @@
             load(hp, t).wait()
             src = (kb, vb, qb)[t]
             acc = None
-            for i in range(4):
-                y = dot(pool[i], src[hp, i * 256:(i + 1) * 256, :])
-                yb = y[:240].astype(BF)
+            ys = {}
+            for step in range(5):
+                if step < 4:
+                    start = 0 if (step < 2) == (t < 2) else 128
+                    ys[step] = (start, dot(pool[step, start:], src[hp, step * 256:(step + 1) * 256, :]))
+                if step == 0:
+                    continue
+                i = step - 1
+                start, y = ys.pop(i)
+                yb = y[:240 - start].astype(BF)
+                mid = 128 - start
+                if start == 0:
+                    if t < 2:
+                        kv1[hp, t, i * 128:(i + 1) * 128, :] = yb[:128]
+                    else:
+                        q1[hp, (i - 2) * 128:(i - 1) * 128, :] = yb[:128]
                 if t < 2:
-                    if i < 2:
-                        kv1[hp, t, i * 128:(i + 1) * 128, :] = yb[:128]
-                    kv2[hp, t, i * 64:(i + 1) * 64, :] = yb[128:192]
-                    kv3[hp, t, i * 32:(i + 1) * 32, :] = yb[192:224]
-                    kv4[hp, t, i * 16:(i + 1) * 16, :] = yb[224:240]
+                    kv2[hp, t, i * 64:(i + 1) * 64, :] = yb[mid:mid + 64]
+                    kv3[hp, t, i * 32:(i + 1) * 32, :] = yb[mid + 64:mid + 96]
+                    kv4[hp, t, i * 16:(i + 1) * 16, :] = yb[mid + 96:mid + 112]
                 else:
-                    if i >= 2:
-                        q1[hp, (i - 2) * 128:(i - 1) * 128, :] = yb[:128]
-                    q2[hp, i * 64:(i + 1) * 64, :] = yb[128:192]
-                    q3[hp, i * 32:(i + 1) * 32, :] = yb[192:224]
-                    q4[hp, i * 16:(i + 1) * 16, :] = yb[224:240]
-                acc = y[240:] if acc is None else acc + y[240:]
+                    q2[hp, i * 64:(i + 1) * 64, :] = yb[mid:mid + 64]
+                    q3[hp, i * 32:(i + 1) * 32, :] = yb[mid + 64:mid + 96]
+                    q4[hp, i * 16:(i + 1) * 16, :] = yb[mid + 96:mid + 112]
+                acc = y[mid + 112:] if acc is None else acc + y[mid + 112:]
             tails.append(acc)
+
+        @pl.when(hp == 0)
+        def _():
+            pl.semaphore_wait(barrier, len(masks))
+
         first = jnp.where(side == 0, tails[0], tails[2]).astype(BF)
         second = tails[1].astype(BF)
         for e in range(2):
@@ -206,22 +267,38 @@
             def _():
                 send_a(h).start()
 
+        return 0
+
+    lax.fori_loop(0, PAIRS, pool_pair, 0)
+
+    def near4(hp, _):
         @pl.when(bit(2) == 0)
         def _():
-            send4(hp, 0).start()
-            send4(hp, 1).start()
-
+            send4(hp).start()
+
+        @pl.when((own & 6) == 2)
+        def _():
+            lend4(hp).start()
+
+        return 0
+
+    def near3(hp, _):
         @pl.when(bit(1) == 0)
         def _():
             send3(hp).start()
 
+        return 0
+
+    def near2(hp, _):
         @pl.when(core == 0)
         def _():
             send2(hp).start()
 
         return 0
 
-    lax.fori_loop(0, PAIRS, pool_pair, 0)
+    lax.fori_loop(0, PAIRS, near2, 0)
+    lax.fori_loop(0, PAIRS, near4, 0)
+    lax.fori_loop(0, 4, near3, 0)
     rt[own] = ts[own]
 
     def wait_a():
@@ -259,18 +336,26 @@
             def _():
                 for i in range(n):
                     copy_b(level, i).wait_recv()
-        terms = []
+        tiles = []
         for level, ref in ((8, r8), (7, r7), (6, r6), (5, r5)):
             start = (0, 256, 384, 448)[level - 5]
             rows = 256 >> (level - 5)
-            terms.append(coarse_term(xs[0, start:start + rows, :], ref[:, 0].reshape(256, HEAD),
-                                     ref[:, 1].reshape(256, HEAD), level, bit(level - 2) == 1))
-        state = terms[0]
-        for term in terms[1:]:
-            state = merge(widen(state, wide.at[0], 2), term)
+            tiles.append(coarse_tile(
+                level, lambda start=start, rows=rows: xs[0, start:start + rows, :],
+                lambda ref=ref: ref[:, 0].reshape(256, HEAD), lambda ref=ref: ref[:, 1].reshape(256, HEAD),
+                bit(level - 2) == 1, lambda *x, start=start, rows=rows: deep.__setitem__(
+                    (slice(None), slice(start, start + rows)), jnp.stack(x))))
+        run_tiles(tiles)
+        deep_of = lambda start, rows: tuple(deep[i, start:start + rows, :] for i in range(3))
+        state = deep_of(448, 32)
+        for start, rows in ((384, 64), (256, 128), (0, 256)):
+            state = merge(widen(state, wide.at[0], 2), deep_of(start, rows))
         lane = lax.broadcasted_iota(jnp.int32, (256, HEAD), 1)
-        cs[:, 0] = state[0].reshape(8, 32, HEAD)
-        cs[:, 1] = jnp.where(lane < 64, state[1], state[2]).reshape(8, 32, HEAD)
+        place = lax.broadcasted_iota(jnp.int32, (256, HEAD), 0) & 31
+        stats = jnp.where(lane == place, state[1], jnp.where(lane == place + 32, state[2], 0.0))
+        stats = jnp.sum(stats.reshape(8, 32, HEAD), axis=1, keepdims=True)
+        cs[:, :32] = state[0].reshape(8, 32, HEAD)
+        cs[:, 32:] = jnp.broadcast_to(stats, (8, 8, HEAD))
         cr[own] = cs[own]
 
         def one(h, _):
@@ -284,25 +369,31 @@
         @pl.when(core == 1)
         def _():
             send2(hp).wait_recv()
+        tiles = []
         for e in range(2):
             cols = slice(e * HEAD, (e + 1) * HEAD)
-            two = coarse_term(q2[hp, :, cols], r2[hp, 0, :, cols], r2[hp, 1, :, cols], 2, core == 1)
-            one = coarse_term(q1[hp, :, cols], kv1[hp, 0, :, cols], kv1[hp, 1, :, cols], 1, None)
-            w = wide.at[e]
-            low = tuple(x[:128] for x in two)
-            high = tuple(x[128:] for x in two)
-            init0 = widen(low, w, 4)
-            init1 = widen(merge(widen(high, w, 2, 512), one), w, 2, 512)
-            for seg, init in ((0, init0), (1, init1)):
-                k = kb[hp, seg * 512:(seg + 1) * 512, cols]
-                v = vb[hp, seg * 512:(seg + 1) * 512, cols]
+            h = 2 * hp + e
+            for seg in range(2):
                 for half in range(2):
-                    at = seg * 512 + half * 256
-                    q = qb[hp, at:at + 256, cols]
-                    part = tuple(x[half * 256:(half + 1) * 256] for x in init)
-                    res = local_block(q, k, v, part, bias[...], half)
-                    for i in range(3):
-                        base[2 * hp + e, i, at:at + 256, :] = res[i]
+                    at, begin = seg * 512 + half * 256, seg * 512
+
+                    def sink(num, peak, total, at=at, h=h):
+                        base[h, 0, at:at + 256, :] = num * (1.0 / total)
+                        lse = peak + jnp.log2(total) * (1.0 / C2)
+                        base[h, 1, at:at + 256, :] = jnp.broadcast_to(lse, num.shape)
+
+                    def parts(ref, begin=begin, half=half, cols=cols):
+                        return [ref[hp, begin + i * 256:begin + (i + 1) * 256, cols] for i in range(half + 1)]
+
+                    tiles.append({"q": lambda at=at, cols=cols: qb[hp, at:at + 256, cols],
+                                  "k": lambda parts=parts: parts(kb), "v": lambda parts=parts: parts(vb),
+                                  "bias": bias, "level": 0, "sink": sink})
+            tiles.append(coarse_tile(1, lambda cols=cols: q1[hp, :, cols], lambda cols=cols: kv1[hp, 0, :, cols],
+                                     lambda cols=cols: kv1[hp, 1, :, cols], None, store(near, h)))
+            tiles.append(coarse_tile(2, lambda cols=cols: q2[hp, :, cols], lambda cols=cols: r2[hp, 0, :, cols],
+                                     lambda cols=cols: r2[hp, 1, :, cols], core == 1, store(far, h)))
+        run_tiles(tiles)
+        forward4(hp)
 
         @pl.when(hp == 0)
         def _():
@@ -332,7 +423,9 @@
         def _():
             @pl.when(bit(2) == 1)
             def _():
-                recv4(step, 0).wait_recv()
+                @pl.when(bit(1) == 0)
+                def _():
+                    recv4(step, 0).wait_recv()
                 recv4(step, 1).wait_recv()
                 relay4(step).start()
 
@@ -353,22 +446,48 @@
             def _():
                 copy_to(r3.at[hp, 1 - core], r3.at[hp, 1 - core], y3.at[hp], z3.at[hp], me ^ 1).wait_recv()
 
+            tiles, threes, fours = [], [None] * 2, [None] * 2
+
+            def keep(into, e):
+                return lambda *x: into.__setitem__(e, x)
+
             for e in range(2):
                 cols = slice(e * HEAD, (e + 1) * HEAD)
+                tiles.append(coarse_tile(
+                    4, lambda cols=cols: q4[hp, :, cols],
+                    lambda cols=cols: r4[hp, :, :, 0, :, cols].reshape(256, HEAD),
+                    lambda cols=cols: r4[hp, :, :, 1, :, cols].reshape(256, HEAD), bit(2) == 1, keep(fours, e)))
+                tiles.append(coarse_tile(
+                    3, lambda cols=cols: q3[hp, :, cols],
+                    lambda cols=cols: r3[hp, :, 0, :, cols].reshape(256, HEAD),
+                    lambda cols=cols: r3[hp, :, 1, :, cols].reshape(256, HEAD), bit(1) == 1, keep(threes, e)))
+            run_tiles(tiles)
+            r32 = lax.broadcasted_iota(jnp.int32, (32, HEAD), 0)
+            l32 = lax.broadcasted_iota(jnp.int32, (32, HEAD), 1)
+            states = []
+            for e in range(2):
                 h = 2 * hp + e
-                w = wide.at[e]
-                three = coarse_term(q3[hp, :, cols], r3[hp, :, 0, :, cols].reshape(256, HEAD),
-                                    r3[hp, :, 1, :, cols].reshape(256, HEAD), 3, bit(1) == 1)
-                four = coarse_term(q4[hp, :, cols], r4[hp, :, :, 0, :, cols].reshape(256, HEAD),
-                                   r4[hp, :, :, 1, :, cols].reshape(256, HEAD), 4, bit(2) == 1)
-                stats = cr[h, 1]
-                five = (cr[h, 0], jnp.broadcast_to(stats[:, :1], (32, HEAD)),
-                        jnp.broadcast_to(stats[:, 64:65], (32, HEAD)))
-                state = merge(widen(five, w, 2), four)
-                state = merge(widen(state, w, 2), three)
-                state = widen(state, w, 8)
-                num, _, total = merge(tuple(base[h, i] for i in range(3)), state)
-                outb[hp, :, cols] = (num / total).astype(BF)
+                stats = jnp.broadcast_to(cr[h, 32:33, :], (32, HEAD))
+                column = lambda at: jnp.broadcast_to(
+                    jnp.sum(jnp.where(l32 == at, stats, 0.0), axis=1, keepdims=True), (32, HEAD))
+                states.append((cr[h, :32, :], column(r32), column(r32 + 32)))
+            for terms in (fours, threes, None):
+                for e in range(2):
+                    term = terms[e] if terms is not None else tuple(far[2 * hp + e, i] for i in range(3))
+                    states[e] = merge(widen(states[e], wide.at[e], 2), term)
+            for e in range(2):
+                h = 2 * hp + e
+                low = tuple(x[:128] for x in states[e])
+                high = tuple(x[128:] for x in states[e])
+                high = merge(widen(high, wide.at[e], 2, 512), tuple(near[h, i] for i in range(3)))
+                for (num, peak, total), times, at in ((low, 4, 0), (high, 2, 512)):
+                    seen = total > 0.0
+                    safe = jnp.where(seen, total, 1.0)
+                    pair = (num * (1.0 / safe), jnp.where(seen, peak + jnp.log2(safe) * (1.0 / C2), NEG))
+                    coarse, lse = widen(pair, wide.at[e], times, at)
+                    fine, fine_lse = base[h, 0, at:at + 512, :], base[h, 1, at:at + 512, :]
+                    share = 1.0 / (1.0 + jnp.exp2((fine_lse - lse) * C2))
+                    outb[hp, at:at + 512, e * HEAD:(e + 1) * HEAD] = (fine + share * (coarse - fine)).astype(BF)
             out_copy(hp).start()
         return 0
 
@@ -391,12 +510,16 @@
 
         @pl.when(bit(2) == 0)
         def _():
-            send4(hp, 0).wait_send()
-            send4(hp, 1).wait_send()
+            send4(hp).wait_send()
+            lend4(hp).wait_send()
 
         @pl.when(bit(2) == 1)
         def _():
             relay4(hp).wait_send()
+
+        @pl.when(own >= 6)
+        def _():
+            hand4(hp).wait_send()
         return 0
 
     lax.fori_loop(0, PAIRS, drain, 0)
@@ -429,15 +552,16 @@
         vm(4, 2, 256, 256), vm(4, 256, 256),
         vm(4, 2, 256, 256), vm(4, 256, 256), vm(4, 2, 256, 256),
         vm(4, 2, 128, 256), vm(4, 128, 256), vm(4, 2, 2, 128, 256),
-        vm(4, 2, 64, 256), vm(4, 64, 256), vm(4, 2, 2, 2, 64, 256),
+        vm(4, 2, 64, 256), vm(4, 64, 256), vm(4, 2, 2, 2, 64, 256), vm(4, 2, 64, 256),
         vm(8, 2, 64, 128), vm(8, 2, 64, 128), vm(2, 512, 128),
         vm(1, 2, 256, 128), vm(2, 2, 128, 128), vm(4, 2, 64, 128), vm(8, 2, 32, 128),
-        vf(8, 2, 32, 128), vf(8, 2, 32, 128),
-        vf(2, 3, 1024, 128), vf(8, 3, 1024, 128), vm(4, 1024, 256),
+        vf(8, 40, 128), vf(8, 40, 128),
+        vf(2, 3, 1024, 128), vf(8, 2, 1024, 128),
+        vf(8, 3, 256, 128), vf(8, 3, 256, 128), vf(3, 480, 128), vm(4, 1024, 256),
         dma(4, 3), dma(4),
         dma(4), dma(4),
         dma(4), dma(4), dma(4), dma(4),
-        dma(4, 2), dma(4, 2), dma(4), dma(4),
+        dma(4, 2), dma(4, 2), dma(4), dma(4), dma(4),
         dma(8), dma(8), dma(15), dma(15), dma(8), dma(8),
     ]
     return pl.pallas_call(

time: 55.1 us -> 43.8 us (0.79)
  Pallas kernels: 47.3 us -> 36 us
    pallas_call x1, Pallas kernels: 47.3 us -> 36 us  [attend(): pl.pallas_call(kernel, out_shape=jax.ShapeDtypeStruct((count, width), BF)...]
where the time goes in v1:
time: 43.8 us; the launch traced here: 43.6 us
  Pallas kernels  36 us (82%)
  matrix products  7.61 us (17%)
    pallas_call x1, Pallas kernels, attend(): pl.pallas_call(kernel, out_shape=jax.ShapeDtypeStruct((count, width), BF)...  36 us
    dot_general x1, matrix products, on_device(): return jnp.dot(attended, w_out, preferred_element_type=F32).astype(BF)  7.61 us

profile of v1, /device:TPU:3, one launch (start us, length us, event | category | flops | bytes accessed | tf_op | source)
XLA Modules:
  0.0 43.6 jit_solution(11881586847558984497)
XLA Ops:
  0.0 0.0 copy-start
  0.0 36.0 %hierarchical_attention.1 = bf16[1024,1024]{1,0:T(8,128)(2,1)} custom-call(bf16[1024,1024]{1,0:T(8,128)(2,1)} %q_hbm.1, bf16[1024,1024]{1,0:T(8,128)(2,1)} %k_hbm.1, bf16[1024,1024]{1,0:T(8,128)(2,1)} %v_hbm.1), custom_call_target="tpu_custom_call" | custom-call | tf_op jit(solution)/shard_map/hierarchical_attention/pallas_call | solution.py:567
  36.0 0.0 copy-done
  36.0 7.6 %convolution_convert_fusion = bf16[1024,2048]{1,0:T(8,128)(2,1)} fusion(bf16[1024,1024]{1,0:T(8,128)(2,1)} %hierarchical_attention.1, bf16[1024,2048]{1,0:T(8,128)(2,1)S(1)} %copy-done), kind=kOutput, calls=%fused_computation | convolution fusion | flops 4297064448 | bytes 10485760 | tf_op jit(solution)/shard_map/dot_general | solution.py:582
Async XLA Ops:
  0.0 36.0 %copy-start = (bf16[1024,2048]{1,0:T(8,128)(2,1)S(1)}, bf16[1024,2048]{1,0:T(8,128)(2,1)}, u32[]{:S(2)}) copy-start(bf16[1024,2048]{1,0:T(8,128)(2,1)} %param.7) | copy-start | bytes 12582916

commit v2 on v1

--- a/solution.py
+++ b/solution.py
@@ -252,10 +252,6 @@
                 acc = y[mid + 112:] if acc is None else acc + y[mid + 112:]
             tails.append(acc)
 
-        @pl.when(hp == 0)
-        def _():
-            pl.semaphore_wait(barrier, len(masks))
-
         first = jnp.where(side == 0, tails[0], tails[2]).astype(BF)
         second = tails[1].astype(BF)
         for e in range(2):
@@ -263,13 +259,16 @@
             ts[h, 0] = first[:, e * HEAD:(e + 1) * HEAD]
             ts[h, 1] = second[:, e * HEAD:(e + 1) * HEAD]
 
-            @pl.when(h != own)
-            def _():
-                send_a(h).start()
-
         return 0
 
     lax.fori_loop(0, PAIRS, pool_pair, 0)
+    pl.semaphore_wait(barrier, len(masks))
+
+    def octet_sends(i, _):
+        send_a((own + i) & 7).start()
+        return 0
+
+    lax.fori_loop(1, 8, octet_sends, 0)
 
     def near4(hp, _):
         @pl.when(bit(2) == 0)
@@ -399,20 +398,12 @@
         def _():
             wait_a()
 
-        @pl.when(hp == 2)
+        @pl.when(hp == 3)
         def _():
             wait_b()
         return 0
 
     lax.fori_loop(0, PAIRS, local_pair, 0)
-
-    def recv_c_all(h, _):
-        @pl.when(h != own)
-        def _():
-            recv_c(h).wait_recv()
-        return 0
-
-    lax.fori_loop(0, 8, recv_c_all, 0)
 
     def out_copy(hp):
         cols = pl.ds(pl.multiple_of(hp * WIDE, WIDE), WIDE)
@@ -462,36 +453,51 @@
                     lambda cols=cols: r3[hp, :, 0, :, cols].reshape(256, HEAD),
                     lambda cols=cols: r3[hp, :, 1, :, cols].reshape(256, HEAD), bit(1) == 1, keep(threes, e)))
             run_tiles(tiles)
-            r32 = lax.broadcasted_iota(jnp.int32, (32, HEAD), 0)
-            l32 = lax.broadcasted_iota(jnp.int32, (32, HEAD), 1)
-            states = []
             for e in range(2):
                 h = 2 * hp + e
-                stats = jnp.broadcast_to(cr[h, 32:33, :], (32, HEAD))
-                column = lambda at: jnp.broadcast_to(
-                    jnp.sum(jnp.where(l32 == at, stats, 0.0), axis=1, keepdims=True), (32, HEAD))
-                states.append((cr[h, :32, :], column(r32), column(r32 + 32)))
-            for terms in (fours, threes, None):
-                for e in range(2):
-                    term = terms[e] if terms is not None else tuple(far[2 * hp + e, i] for i in range(3))
-                    states[e] = merge(widen(states[e], wide.at[e], 2), term)
-            for e in range(2):
-                h = 2 * hp + e
-                low = tuple(x[:128] for x in states[e])
-                high = tuple(x[128:] for x in states[e])
-                high = merge(widen(high, wide.at[e], 2, 512), tuple(near[h, i] for i in range(3)))
-                for (num, peak, total), times, at in ((low, 4, 0), (high, 2, 512)):
-                    seen = total > 0.0
-                    safe = jnp.where(seen, total, 1.0)
-                    pair = (num * (1.0 / safe), jnp.where(seen, peak + jnp.log2(safe) * (1.0 / C2), NEG))
-                    coarse, lse = widen(pair, wide.at[e], times, at)
-                    fine, fine_lse = base[h, 0, at:at + 512, :], base[h, 1, at:at + 512, :]
-                    share = 1.0 / (1.0 + jnp.exp2((fine_lse - lse) * C2))
-                    outb[hp, at:at + 512, e * HEAD:(e + 1) * HEAD] = (fine + share * (coarse - fine)).astype(BF)
-            out_copy(hp).start()
+                state = merge(widen(fours[e], wide.at[e], 2), threes[e])
+                state = merge(widen(state, wide.at[e], 2), tuple(far[h, i] for i in range(3)))
+                store(far, h)(*state)
         return 0
 
     lax.fori_loop(0, PAIRS + 1, final_pair, 0)
+
+    def recv_c_all(h, _):
+        @pl.when(h != own)
+        def _():
+            recv_c(h).wait_recv()
+        return 0
+
+    lax.fori_loop(0, 8, recv_c_all, 0)
+
+    def last_pair(hp, _):
+        r32 = lax.broadcasted_iota(jnp.int32, (32, HEAD), 0)
+        l32 = lax.broadcasted_iota(jnp.int32, (32, HEAD), 1)
+        states = []
+        for e in range(2):
+            h = 2 * hp + e
+            stats = jnp.broadcast_to(cr[h, 32:33, :], (32, HEAD))
+            column = lambda at: jnp.broadcast_to(
+                jnp.sum(jnp.where(l32 == at, stats, 0.0), axis=1, keepdims=True), (32, HEAD))
+            state = widen((cr[h, :32, :], column(r32), column(r32 + 32)), wide.at[e], 8)
+            states.append(merge(state, tuple(far[h, i] for i in range(3))))
+        for e in range(2):
+            h = 2 * hp + e
+            low = tuple(x[:128] for x in states[e])
+            high = tuple(x[128:] for x in states[e])
+            high = merge(widen(high, wide.at[e], 2, 512), tuple(near[h, i] for i in range(3)))
+            for (num, peak, total), times, at in ((low, 4, 0), (high, 2, 512)):
+                seen = total > 0.0
+                safe = jnp.where(seen, total, 1.0)
+                pair = (num * (1.0 / safe), jnp.where(seen, peak + jnp.log2(safe) * (1.0 / C2), NEG))
+                coarse, lse = widen(pair, wide.at[e], times, at)
+                fine, fine_lse = base[h, 0, at:at + 512, :], base[h, 1, at:at + 512, :]
+                share = 1.0 / (1.0 + jnp.exp2((fine_lse - lse) * C2))
+                outb[hp, at:at + 512, e * HEAD:(e + 1) * HEAD] = (fine + share * (coarse - fine)).astype(BF)
+        out_copy(hp).start()
+        return 0
+
+    lax.fori_loop(0, PAIRS, last_pair, 0)
 
     def drain(hp, _):
         out_copy(hp).wait()
@@ -571,7 +577,7 @@
         out_specs=pl.BlockSpec(memory_space=pl.ANY),
         scratch_shapes=scratch,
         compiler_params=pltpu.CompilerParams(
-            collective_id=0, has_side_effects=True, vmem_limit_bytes=56 * 1024 * 1024
+            collective_id=0, has_side_effects=True, vmem_limit_bytes=50 * 1024 * 1024
         ),
         name="hierarchical_attention",
     )(queries, keys, values)

time: 43.8 us -> 38.2 us (0.87)
  Pallas kernels: 36 us -> 32 us
  matrix products: 7.61 us -> 6.02 us
    pallas_call x1, Pallas kernels: 36 us -> 32 us  [attend(): pl.pallas_call(kernel, out_shape=jax.ShapeDtypeStruct((count, width), BF)...]
    dot_general x1, matrix products: 7.61 us -> 6.02 us  [on_device(): return jnp.dot(attended, w_out, preferred_element_type=F32).astype(BF)]
where the time goes in v2:
time: 38.2 us; the launch traced here: 38 us
  Pallas kernels  32 us (84%)
  matrix products  6.02 us (16%)
    pallas_call x1, Pallas kernels, attend(): pl.pallas_call(kernel, out_shape=jax.ShapeDtypeStruct((count, width), BF)...  32 us
    dot_general x1, matrix products, on_device(): return jnp.dot(attended, w_out, preferred_element_type=F32).astype(BF)  6.02 us

profile of v2, /device:TPU:3, one launch (start us, length us, event | category | flops | bytes accessed | tf_op | source)
XLA Modules:
  0.0 38.0 jit_solution(10466715094820207562)
XLA Ops:
  0.0 0.0 copy-start
  0.0 32.0 %hierarchical_attention.1 = bf16[1024,1024]{1,0:T(8,128)(2,1)S(1)} custom-call(bf16[1024,1024]{1,0:T(8,128)(2,1)} %q_hbm.1, bf16[1024,1024]{1,0:T(8,128)(2,1)} %k_hbm.1, bf16[1024,1024]{1,0:T(8,128)(2,1)} %v_hbm.1), custom_call_target="tpu_custom_call" | custom-call | tf_op jit(solution)/shard_map/hierarchical_attention/pallas_call | solution.py:573
  32.0 0.0 copy-done
  32.0 6.0 %convolution_convert_fusion = bf16[1024,2048]{1,0:T(8,128)(2,1)} fusion(bf16[1024,1024]{1,0:T(8,128)(2,1)S(1)} %hierarchical_attention.1, bf16[1024,2048]{1,0:T(8,128)(2,1)S(1)} %copy-done), kind=kOutput, calls=%fused_computation | convolution fusion | flops 4297064448 | bytes 10485760 | tf_op jit(solution)/shard_map/dot_general | solution.py:588
Async XLA Ops:
  0.0 32.0 %copy-start = (bf16[1024,2048]{1,0:T(8,128)(2,1)S(1)}, bf16[1024,2048]{1,0:T(8,128)(2,1)}, u32[]{:S(2)}) copy-start(bf16[1024,2048]{1,0:T(8,128)(2,1)} %param.7) | copy-start | bytes 12582916

commit v3 on v2

--- a/solution.py
+++ b/solution.py
@@ -219,7 +219,18 @@
         mask = 8 * (n + i)
         return copy_to(xs.at[:, pl.ds(start, count)], dst.at[i], sb.at[slot], gb.at[slot], me ^ mask)
 
+    def octet_sends(h, _):
+        @pl.when(h != own)
+        def _():
+            send_a(h).start()
+        return 0
+
     def pool_pair(hp, _):
+        @pl.when(hp == 3)
+        def _():
+            pl.semaphore_wait(barrier, len(masks))
+            lax.fori_loop(0, 6, octet_sends, 0)
+
         tails = []
         for t in range(3):
             load(hp, t).wait()
@@ -262,13 +273,7 @@
         return 0
 
     lax.fori_loop(0, PAIRS, pool_pair, 0)
-    pl.semaphore_wait(barrier, len(masks))
-
-    def octet_sends(i, _):
-        send_a((own + i) & 7).start()
-        return 0
-
-    lax.fori_loop(1, 8, octet_sends, 0)
+    lax.fori_loop(6, 8, octet_sends, 0)
 
     def near4(hp, _):
         @pl.when(bit(2) == 0)

time: 38.2 us -> 38.6 us (1.010)
  no operation moved by 1% of the time
where the time goes in v3:
time: 38.6 us; the launch traced here: 38.3 us
  Pallas kernels  32.3 us (84%)
  matrix products  6.02 us (16%)
    pallas_call x1, Pallas kernels, attend(): pl.pallas_call(kernel, out_shape=jax.ShapeDtypeStruct((count, width), BF)...  32.3 us
    dot_general x1, matrix products, on_device(): return jnp.dot(attended, w_out, preferred_element_type=F32).astype(BF)  6.02 us

profile of v3, /device:TPU:3, one launch (start us, length us, event | category | flops | bytes accessed | tf_op | source)
XLA Modules:
  0.0 38.3 jit_solution(16259509483177880315)
XLA Ops:
  0.0 0.0 copy-start
  0.0 32.3 %hierarchical_attention.1 = bf16[1024,1024]{1,0:T(8,128)(2,1)S(1)} custom-call(bf16[1024,1024]{1,0:T(8,128)(2,1)} %q_hbm.1, bf16[1024,1024]{1,0:T(8,128)(2,1)} %k_hbm.1, bf16[1024,1024]{1,0:T(8,128)(2,1)} %v_hbm.1), custom_call_target="tpu_custom_call" | custom-call | tf_op jit(solution)/shard_map/hierarchical_attention/pallas_call | solution.py:578
  32.3 0.0 copy-done
  32.3 6.0 %convolution_convert_fusion = bf16[1024,2048]{1,0:T(8,128)(2,1)} fusion(bf16[1024,1024]{1,0:T(8,128)(2,1)S(1)} %hierarchical_attention.1, bf16[1024,2048]{1,0:T(8,128)(2,1)S(1)} %copy-done), kind=kOutput, calls=%fused_computation | convolution fusion | flops 4297064448 | bytes 10485760 | tf_op jit(solution)/shard_map/dot_general | solution.py:593
Async XLA Ops:
  0.0 32.3 %copy-start = (bf16[1024,2048]{1,0:T(8,128)(2,1)S(1)}, bf16[1024,2048]{1,0:T(8,128)(2,1)}, u32[]{:S(2)}) copy-start(bf16[1024,2048]{1,0:T(8,128)(2,1)} %param.7) | copy-start | bytes 12582916
